TPU v7x, 128 devices: a whole 4x4x4 slice. The times are simulated.
128 devices in a mesh: row: 8 (over y_lo, z), col: 16 (over y_hi, x, core).
Axes of the slice: x: 4, y: 4 (y_hi: 2, y_lo: 2; y = y_hi * 2 + y_lo), z: 4, core: 2. Of those that a mesh axis runs over, the one named last changes fastest.
Arguments:
- images: bfloat16 [65536, 2, 4096], P(('row', 'col')), may hold values from -320 to 320
- precision: float32 [65536], P(('row', 'col')), may hold values from 0.001 to 0.01
- templates: bfloat16 [128, 2, 4096], P(('row', 'col')), may hold values from -4 to 4
- template_id: int32 [128], replicated, may hold values from 0 to 127, as said below
- shift_table: int32 [128, 8], replicated, may hold values from 0 to 63, as said below
Outputs:
- updated: float32 [128, 2, 4096], P(('row', 'col'))
Inputs may be any that keep to these rules, and one draw needn't show every extreme that they name: `template_id`: A permutation of 0 to 127. `shift_table`: each row holds 8 different shift numbers.
All inputs are finite; a program needn't handle non-finite values.
Results may differ from a plain program's by a relative error of at most 0.00058.
Values may be sent and summed in bfloat16 or wider, within the bound.
A program may use at most 192 MiB of HBM per device.

v0:
```python
import math

import jax
import jax.numpy as jnp
from jax import lax
from jax.sharding import PartitionSpec as P

GRID = 64


PRIOR_WEIGHT = 4.0


def phase_tables(grid_side):
    coefficient = jnp.arange(grid_side * grid_side, dtype=jnp.int32)
    freq_x = coefficient // grid_side - grid_side // 2
    freq_y = coefficient % grid_side - grid_side // 2
    shift_number = jnp.arange(64, dtype=jnp.int32)
    step_x = shift_number // 8 - 4
    step_y = shift_number % 8 - 4
    phase_index = (
        step_x[:, None] * freq_x[None, :] + step_y[:, None] * freq_y[None, :]
    ) % grid_side
    angle_value = phase_index.astype(jnp.float32) * (2.0 * math.pi / grid_side)
    return (jnp.cos(angle_value), jnp.sin(angle_value))


def shift_forward(real_part, imag_part, cosine, sine_table):
    return (
        real_part * cosine + imag_part * sine_table,
        imag_part * cosine - real_part * sine_table,
    )


def shift_back(real_part, imag_part, cosine, sine_table):
    return (
        real_part * cosine - imag_part * sine_table,
        imag_part * cosine + real_part * sine_table,
    )


def body(images, precision, templates, template_id, shift_table):
    image_count = images.shape[0]
    coeffs = images.shape[2]
    local_count = templates.shape[0]
    shifts_each = shift_table.shape[1]
    row_count = lax.axis_size("row")
    col_count = lax.axis_size("col")
    template_count = local_count * row_count * col_count
    cos_table, sin_table = phase_tables(GRID)
    flat_images = images.reshape(image_count, 2 * coeffs)

    def shift_parts(positions):
        shift_rows = shift_table[template_id[positions]]
        return (cos_table[shift_rows], sin_table[shift_rows])

    pieces = lax.all_gather(templates, ("row", "col"), axis=0, tiled=True)
    how_many = pieces.shape[0]
    positions = jnp.arange(how_many, dtype=jnp.int32)
    cosine, sine_table = shift_parts(positions)
    template_f = pieces.astype(jnp.float32)
    real_part, imag_part = shift_forward(
        template_f[:, None, 0], template_f[:, None, 1], cosine, sine_table
    )
    rotated = (
        jnp.stack([real_part, imag_part], axis=2)
        .astype(jnp.bfloat16)
        .reshape(how_many * shifts_each, 2 * coeffs)
    )
    half_norm = jnp.repeat(0.5 * jnp.sum(template_f * template_f, axis=(1, 2)), shifts_each)
    inner_products = lax.dot_general(
        flat_images, rotated, (((1,), (1,)), ((), ())), preferred_element_type=jnp.float32
    )
    scores = precision[:, None] * (inner_products - half_norm[None, :])
    highest = jnp.max(scores, axis=1, keepdims=True)
    exponent = jnp.exp(scores - highest)
    weights = (exponent / jnp.sum(exponent, axis=1, keepdims=True)).astype(jnp.bfloat16)
    accumulated = lax.dot_general(
        weights, flat_images, (((0,), (0,)), ((), ())), preferred_element_type=jnp.float32
    )
    accumulated = accumulated.reshape(
        local_count * lax.axis_size(("row", "col")), shifts_each, 2, coeffs
    )
    positions = jnp.arange(local_count * lax.axis_size(("row", "col")), dtype=jnp.int32)
    cosine, sine_table = shift_parts(positions)
    back_real, back_imag = shift_back(
        accumulated[:, :, 0], accumulated[:, :, 1], cosine, sine_table
    )
    summed = lax.psum_scatter(
        jnp.stack([jnp.sum(back_real, axis=1), jnp.sum(back_imag, axis=1)], axis=1),
        ("row", "col"),
        scatter_dimension=0,
        tiled=True,
    )
    weight_sums = jnp.sum(
        jnp.sum(weights, axis=0, dtype=jnp.float32).reshape(template_count, shifts_each), axis=1
    )
    all_totals = lax.psum(weight_sums, ("row", "col"))
    own_block = lax.axis_index("row") * col_count + lax.axis_index("col")
    own_totals = lax.dynamic_slice_in_dim(all_totals, own_block * local_count, local_count, 0)
    template_f = templates.astype(jnp.float32)
    return (summed + PRIOR_WEIGHT * template_f) / (own_totals + PRIOR_WEIGHT)[:, None, None]


def solution(mesh):
    return jax.shard_map(
        body,
        mesh=mesh,
        in_specs=(
            P(("row", "col"), None, None),
            P(("row", "col")),
            P(("row", "col"), None, None),
            P(),
            P(),
        ),
        out_specs=P(("row", "col"), None, None),
        check_vma=False,
    )
```

profile of v0, /device:TPU:0, one launch (start us, length us, event | category | flops | bytes accessed | tf_op | source)
XLA Modules:
  0.0 481.9 jit_solution(17194872067008503977)
XLA Ops:
  6.5 0.0 copy-start
  6.5 0.0 all-gather.2.cloned.1.call-start
  6.5 0.7 all-gather.2.cloned.1.call-update
  7.3 0.0 all-reduce.3.cloned.1.call-start
  7.3 0.8 copy.40
  8.1 0.0 copy-done
  8.1 1.2 gather_fusion
  9.4 0.6 gather_fusion.1
  10.0 0.1 reshape.153
  10.2 4.2 fusion.12
  14.4 9.1 %gather_fusion.2 = f32[1024,4096]{1,0:T(8,128)} fusion(f32[64,4096]{1,0:T(8,128)S(1)} %get-tuple-element.13, s32[1024]{0:T(1024)S(1)} %broadcast_clamp_fusion), kind=kCustom, calls=%fused_computation.2 | custom fusion | bytes 33558528 | tf_op jit(solution)/shard_map/gather | solution.py:55
  23.5 9.6 %gather_fusion.3 = f32[1024,4096]{1,0:T(8,128)} fusion(f32[64,4096]{1,0:T(8,128)S(1)} %get-tuple-element.14, s32[1024]{0:T(1024)S(1)} %broadcast_clamp_fusion), kind=kCustom, calls=%fused_computation.3 | custom fusion | bytes 33558528 | tf_op jit(solution)/shard_map/gather | solution.py:55
  33.1 16.2 %copy.53 = bf16[64,8,2,4096]{3,1,2,0:T(8,128)(2,1)} copy(bf16[64,8,2,4096]{3,2,1,0:T(2,128)(2,1)} %bitcast.68) | data formatting | bytes 16777216
  49.3 12.1 %copy.41 = bf16[8192,512]{1,0:T(8,128)(2,1)} copy(bf16[8192,512]{0,1:T(8,128)(2,1)} %bitcast.65) | data formatting | bytes 16777216 | tf_op jit(solution)/shard_map/dot_general | solution.py:78
  61.4 144.6 %all-gather.2.cloned.1.call-done = bf16[128,2,4096]{2,1,0:T(2,128)(2,1)} async-done(((bf16[1,2,4096]{2,1,0:T(2,128)(2,1)}), bf16[128,2,4096]{2,1,0:T(2,128)(2,1)}) %all-gather.2.cloned.1.call-update) | async-done | bytes 2097168 | tf_op jit(solution)/shard_map/all_gather | solution.py:57
  206.0 0.0 copy-start.2
  206.0 3.4 copy_convert_fusion
  209.4 1.7 slice_bitcast_fusion.3
  211.2 0.0 copy-done.2
  211.2 1.7 multiply_reduce_fusion
  212.9 0.1 broadcast_in_dim.2
  213.0 0.1 sub.78
  213.1 16.0 %fusion.1 = (bf16[128,8,1,4096]{3,1,2,0:T(8,128)(2,1)S(1)}, bf16[128,8,1,4096]{3,1,2,0:T(8,128)(2,1)}) fusion(f32[1024,4096]{1,0:T(8,128)} %gather_fusion.3, f32[1024,4096]{1,0:T(8,128)} %gather_fusion.2, f32[128,4096]{1,0:T(8,128)} %get-tuple-element.12, f32[128,4096]{1,0:T(8,128)S(1)} %get-tuple-element.11), kind=kLoop, calls=%fused_computation.10 | loop fusion | flops 33554432 | bytes 54525952 | tf_op jit(solution)/shard_map/convert
  229.0 0.0 copy-start.4
  229.1 10.5 %pad_maximum_fusion = bf16[128,8,2,4096]{3,1,2,0:T(8,128)(2,1)} fusion(bf16[128,8,1,4096]{3,1,2,0:T(8,128)(2,1)} %get-tuple-element.10, bf16[128,8,1,4096]{3,1,2,0:T(8,128)(2,1)S(1)} %get-tuple-element.9), kind=kLoop, calls=%fused_computation.6 | loop fusion | flops 8388608 | bytes 33554432 | tf_op jit(solution)/shard_map/stack | solution.py:66
  239.6 0.0 copy-done.4
  239.6 14.5 %fusion.4 = (f32[512]{0:T(512)S(1)}, f32[1024,512]{1,0:T(8,128)S(1)}) fusion(f32[1024]{0:T(1024)S(1)} %sub.78, f32[512]{0:T(512)S(1)} %copy-done.4, bf16[1024,8192]{1,0:T(8,128)(2,1)} %bitcast.67, bf16[512,8192]{1,0:T(8,128)(2,1)} %bitcast.66), kind=kOutput, calls=%fused_computation.26 | convolution fusion | flops 8591507456 | bytes 27271168 | tf_op jit(solution)/shard_map/dot_general | solution.py:71
  254.1 0.5 fusion.5
  254.6 0.7 convert_reduce_fusion
  255.2 18.9 %fusion.9 = f32[128,8,2,4096]{3,0,2,1:T(8,128)} fusion(bf16[2,4096,512,1]{2,1,0,3:T(8,128)(2,1)} %bitcast.69, bf16[128,8,512,1]{2,1,0,3:T(8,128)(2,1)S(1)} %bitcast.72), kind=kOutput, calls=%fused_computation.34 | convolution fusion | flops 8589934592 | bytes 42991616 | tf_op jit(solution)/shard_map/dot_general | solution.py:78
  274.2 40.8 %subtract_reduce_fusion = (f32[128,4096]{1,0:T(8,128)S(1)}, f32[128,4096]{1,0:T(8,128)S(1)}) fusion(f32[128,8,2,4096]{3,0,2,1:T(8,128)} %fusion.9, f32[128,8,4096]{2,1,0:T(8,128)} %bitcast.64, f32[128,8,4096]{2,1,0:T(8,128)} %bitcast.63), kind=kLoop, calls=%fused_computation.16 | loop fusion | flops 32505856 | bytes 71303168 | tf_op jit(solution)/shard_map/reduce_sum | solution.py:90
  314.9 0.0 copy-start.1
  314.9 0.3 pad_maximum_fusion.1
  315.2 0.0 copy-start.3
  315.2 5.2 %copy.48 = f32[128,2,4096]{2,1,0:T(2,128)} copy(f32[128,2,4096]{2,0,1:T(8,128)S(1)} %pad_maximum_fusion.1) | data formatting | bytes 8388608 | tf_op jit(solution)/shard_map/stack | solution.py:90
  320.4 0.0 all-reduce.3.cloned.1.call-update
  320.5 0.1 reshape.134
  320.6 0.1 reduce_sum.59
  320.7 63.0 %psum.7 = f32[128]{0:T(128)S(1)} all-reduce(f32[128]{0:T(128)S(1)} %reduce_sum.59), channel_id=1, replica_groups=mesh['row'=8,'col'=16] {'row','col'}, use_global_device_ids=true, to_apply=%region_8.9 | all-reduce | flops 128 | bytes 1024 | tf_op jit(solution)/shard_map/psum | solution.py:98
  383.7 0.6 dynamic_slice.3
  384.9 88.5 %all-reduce.3.cloned.1.call-done = f32[128,2,4096]{2,1,0:T(2,128)} async-done(((f32[128,2,4096]{2,1,0:T(2,128)}), f32[128,2,4096]{2,1,0:T(2,128)}) %all-reduce.3.cloned.1.call-update) | async-done | bytes 4194320
  473.4 0.0 copy-done.3
  473.4 1.4 fusion.13
  474.8 0.0 copy-done.1
  (9 shorter events, 0.1 us)
Async XLA Ops:
  6.5 1.6 copy-start
  6.5 199.5 %all-gather.2.cloned.1.call-start = ((), (), s32[]{:S(2)}) async-start(), calls=%async_computation | async-start | bytes 2113536 | tf_op jit(solution)/shard_map/all_gather | solution.py:57
  7.3 466.1 %all-reduce.3.cloned.1.call-start = ((), (), s32[]{:S(2)}) async-start(), calls=%async_computation.1 | async-start | bytes 8388608
  206.0 5.1 %copy-start.2 = (bf16[128,2,4096]{2,1,0:T(2,128)(2,1)S(1)}, bf16[128,2,4096]{2,1,0:T(2,128)(2,1)}, u32[]{:S(2)}) copy-start(bf16[128,2,4096]{2,1,0:T(2,128)(2,1)} %all-gather.2.cloned.1.call-done) | copy-start | bytes 6291460
  229.0 10.5 %copy-start.4 = (f32[512]{0:T(512)S(1)}, f32[512]{0:T(512)}, u32[]{:S(2)}) copy-start(f32[512]{0:T(512)} %param.6) | copy-start | bytes 6148
  314.9 159.8 %copy-start.1 = (s32[128]{0:T(128)S(1)}, s32[128]{0:T(128)}, u32[]{:S(2)}) copy-start(s32[128]{0:T(128)} %param.8) | copy-start | bytes 1540
  315.2 158.1 %copy-start.3 = (bf16[1,2,4096]{2,1,0:T(2,128)(2,1)S(1)}, bf16[1,2,4096]{2,1,0:T(2,128)(2,1)}, u32[]{:S(2)}) copy-start(bf16[1,2,4096]{2,1,0:T(2,128)(2,1)} %param.7) | copy-start | bytes 49156
Sparse Core Ops, SparseCore 0:
  9.1 196.8 all-gather.1
  320.6 152.7 all-reduce.2
where the time goes:
time: 488 us; the launch traced here: 482 us
  waiting for transfers between devices  234 us (48%)
  other arithmetic  79.6 us (16%)
  blocking collectives  63 us (13%)
  local copies, waits for them, and re-layouts  57.6 us (12%)
  matrix products  33.4 us (7%)
  between operations  14.5 us (3%)
    all_gather x1, waiting for transfers between devices, body(): pieces = lax.all_gather(templates, ('row', 'col'), axis=0, tiled=True)  145 us
    unnamed x3, waiting for transfers between devices  89.2 us
    psum x1, blocking collectives, body(): all_totals = lax.psum(weight_sums, ('row', 'col'))  63 us
    reduce_sum x1, other arithmetic, body(): jnp.sum(back_real, axis=1)  40.8 us
    dot_general x1, matrix products, body(): lax.dot_general(weights, flat_images, (((0,), (0,)), ((), ())), preferred...  18.9 us
    gather x2, local copies, waits for them, and re-layouts, shift_parts(): return (cos_table[shift_rows], sin_table[shift_rows])  18.7 us
    unnamed x12, local copies, waits for them, and re-layouts  17 us
    another operation x1, other arithmetic  16 us
  transfers between devices with their start and end apart: 2, of which 2 were waited for; matrix products, arithmetic and copies ran while one was open for 11% of the time, Pallas kernels for 0%

commit v1 on v0

v1 whole, which is shorter than its diff:
```python
import functools

import jax
import jax.numpy as jnp
import ml_dtypes
import numpy as np
from jax import lax
from jax.experimental import pallas as pl
from jax.experimental.pallas import tpu as pltpu
from jax.sharding import PartitionSpec as P

MESH = pl.DeviceIdType.MESH
F32 = jnp.float32
BF16 = jnp.bfloat16

GRID = 64
COEFFS = 4096
TEMPLATES = 128
SHIFTS = 8
PAIRS = TEMPLATES * SHIFTS
N_IMG = 512
ROWS = 64
ROWS_ALL = 72
STEP = 512
STEPS = 2 * COEFFS // STEP
PRIOR_WEIGHT = 4.0
MIB = 1 << 20

ORDERS = ((2, 1, 0), (1, 0, 2), (0, 2, 1))


def phase_constant():
    c = np.arange(COEFFS)
    fx = c // GRID - GRID // 2
    fy = c % GRID - GRID // 2
    s = np.arange(64)
    k = ((s // 8 - 4)[:, None] * fx[None] + (s % 8 - 4)[:, None] * fy[None]) % GRID
    angle = k * (2.0 * np.pi / GRID)
    both = np.stack([np.cos(angle), np.sin(angle)], 1).reshape(64, 2, 32, 128)
    both = both.transpose(0, 2, 1, 3).reshape(64, 2 * COEFFS).astype(np.float32)
    high = both.astype(ml_dtypes.bfloat16)
    rest = both - high.astype(np.float32)
    mid = rest.astype(ml_dtypes.bfloat16)
    low = (rest - mid.astype(np.float32)).astype(ml_dtypes.bfloat16)
    return np.concatenate([high, mid, low], 0)


def place():
    row, col = lax.axis_index("row"), lax.axis_index("col")
    z, y_lo = row % 4, row // 4
    core, x, y_hi = col % 2, (col // 2) % 4, col // 8
    return core, (z, y_hi * 2 + y_lo, x)


def device(core, at):
    z, y, x = at
    return ((y % 2) * 4 + z, ((y // 2) * 4 + x) * 2 + core)


def moved(at, axis, by):
    return tuple((v + by) % 4 if i == axis else v for i, v in enumerate(at))


def enter(core, at):
    barrier = pltpu.get_barrier_semaphore()
    others = [device(1 - core, at)]
    others += [device(core, moved(at, a, d)) for a in range(3) for d in (1, 2, 3)]
    for other in others:
        pl.semaphore_signal(barrier, inc=1, device_id=other, device_id_type=MESH)
    pl.semaphore_wait(barrier, len(others))


def gather_kernel(t_ref, g_ref, send_sem, recv_sem):
    core, at = place()
    enter(core, at)
    g_ref[core, at[0], at[1], at[2]] = t_ref[...]
    groups = [(pl.ds(16 * g, 16), (ORDERS + ORDERS)[g]) for g in range(4)]

    def view(rows, order, stage, where):
        done = order[:stage]
        index = tuple(slice(None) if a in done else where[a] for a in range(3))
        return g_ref.at[(core,) + index + (rows,)]

    def copy(g, stage, d, arrived=False):
        rows, order = groups[g]
        if stage == 3:
            ref = g_ref.at[1 - core if arrived else core, :, :, :, rows]
            target = device(1 - core, at)
        else:
            axis = order[stage]
            ref = view(rows, order, stage, moved(at, axis, 4 - d) if arrived else at)
            target = device(core, moved(at, axis, d))
        return pltpu.make_async_remote_copy(
            src_ref=ref, dst_ref=ref, send_sem=send_sem.at[g, stage, d - 1],
            recv_sem=recv_sem.at[g, stage, d - 1], device_id=target, device_id_type=MESH)

    def each(stage):
        return (1, 3, 2) if stage < 3 else (1,)

    for stage in range(4):
        for g in range(4):
            if stage:
                for d in each(stage - 1):
                    copy(g, stage - 1, d, True).wait_recv()
            for d in each(stage):
                copy(g, stage, d).start()
    for g in range(4):
        copy(g, 3, 1, True).wait_recv()
    for stage in range(4):
        for g in range(4):
            for d in each(stage):
                copy(g, stage, d).wait_send()


def scatter_kernel(p_in, t_ref, out_ref, p_ref, r0, r1, r2, r3, send_sem, recv_sem, load_sem):
    core, at = place()
    load = pltpu.make_async_copy(p_in, p_ref, load_sem)
    load.start()
    enter(core, at)
    load.wait()
    lands = (r0, r1, r2, r3)

    def kept(order, stage):
        return (core,) + tuple(at[a] if a in order[:stage] else slice(None) for a in range(3))

    def copy(k, o, stage, d):
        rows = pl.ds(pl.multiple_of(k * 8, 8), 8)
        order = ORDERS[o]
        if stage == 0:
            src = p_ref.at[1 - core, :, :, :, rows]
            dst = r0.at[:, :, :, rows]
            target = device(1 - core, at)
        else:
            axis = order[stage - 1]
            other = moved(at, axis, d)
            index = [at[a] if a in order[:stage - 1] else slice(None) for a in range(3)]
            index[axis] = other[axis]
            src = p_ref.at[(core,) + tuple(index) + (rows,)]
            dst = lands[stage].at[(d - 1,) + (slice(None),) * (3 - stage) + (rows,)]
            target = device(core, other)
        return pltpu.make_async_remote_copy(
            src_ref=src, dst_ref=dst, send_sem=send_sem.at[k, stage, d - 1],
            recv_sem=recv_sem.at[k, stage, d - 1], device_id=target, device_id_type=MESH)

    def each(stage):
        return (1, 3, 2) if stage else (1,)

    def take(k, o, stage):
        rows = pl.ds(pl.multiple_of(k * 8, 8), 8)
        for d in each(stage):
            copy(k, o, stage, d).wait_recv()
        index = kept(ORDERS[o], stage) + (rows,)
        total = p_ref[index]
        if stage == 0:
            total += r0[:, :, :, rows]
        else:
            for d in (1, 2, 3):
                total += lands[stage][(d - 1,) + (slice(None),) * (3 - stage) + (rows,)]
        p_ref[index] = total

    for stage in range(4):
        @pl.loop(0, 3)
        def _(kk):
            for o in range(3):
                k = kk * 3 + o
                if stage:
                    take(k, o, stage - 1)
                for d in each(stage):
                    copy(k, o, stage, d).start()

    @pl.loop(0, 3)
    def _(kk):
        for o in range(3):
            take(kk * 3 + o, o, 3)

    @pl.loop(0, 3)
    def _(kk):
        for o in range(3):
            for stage in range(4):
                for d in each(stage):
                    copy(kk * 3 + o, o, stage, d).wait_send()

    own = p_ref[core, at[0], at[1], at[2]]
    total = jnp.sum(own[ROWS:], keepdims=True) + PRIOR_WEIGHT
    out_ref[...] = (own[:ROWS] + PRIOR_WEIGHT * t_ref[...].astype(F32)) / total


def compute_kernel(img, tab, g_ref, prec, tid, table, p_ref,
                   x, raw, wide, fac, acc, rot, wt, onehot, norm, tabs, img_sem, tab_sem):
    def fetch(b):
        return pltpu.make_async_copy(img.at[pl.ds(b * 4096, 4096)], raw.at[b % 2], img_sem.at[b % 2])

    def fetch_tab(k, slot):
        return pltpu.make_async_copy(
            tab.at[:, pl.ds(pl.multiple_of(k * STEP, STEP), STEP)], tabs.at[slot], tab_sem.at[slot])

    fetch(0).start()
    for b in range(8):
        if b < 7:
            fetch(b + 1).start()
        fetch(b).wait()
        wide[pl.ds(0, 4096)] = raw[b % 2].astype(F32)

        @pl.loop(0, ROWS)
        def _(r):
            lanes = pl.ds(pl.multiple_of(r * 128, 128), 128)
            x[pl.ds(b * 64, 64), lanes] = wide[pl.ds(r, 64, stride=ROWS), :].astype(BF16)

    ids = lax.broadcasted_iota(jnp.int32, (128, 128), 0)
    pick = jnp.where(ids == tid[...], 1.0, 0.0).astype(BF16)
    shifts_t = jnp.dot(table[...].astype(F32).astype(BF16), pick, preferred_element_type=F32)
    slot = lax.broadcasted_iota(jnp.int32, (128, 128), 1)
    row, col = slot // 16, slot % 16
    inner = (col % 2) * 64 + (row % 4) * 16 + ((col // 8) * 2 + row // 4) * 4 + (col // 2) % 4
    perm = jnp.where(ids == inner, 1.0, 0.0).astype(BF16)
    shifts = lax.dot_general(perm, shifts_t.astype(BF16), (((1,), (1,)), ((), ())),
                             preferred_element_type=F32)
    lane = lax.broadcasted_iota(jnp.int32, (128, 64), 1).astype(F32)
    for j in range(SHIFTS):
        one = jnp.where(lane == shifts[:, j:j + 1], 1.0, 0.0).astype(BF16)
        onehot[pl.ds(j * 128, 128), :] = jnp.concatenate([one, one, one], axis=1)

    @pl.loop(0, TEMPLATES)
    def _(p):
        wide[pl.ds(pl.multiple_of(p * ROWS, ROWS), ROWS)] = g_ref[p].astype(F32)

    @pl.loop(0, TEMPLATES // 8)
    def _(b):
        def add(r, total):
            t = wide[pl.ds(b * 8 * ROWS + r, 8, stride=ROWS), :]
            return total + t * t
        total = lax.fori_loop(0, ROWS, add, jnp.zeros((8, 128), F32), unroll=8)
        norm[pl.ds(pl.multiple_of(b * 8, 8), 8), :] = jnp.broadcast_to(
            0.5 * jnp.sum(total, axis=1, keepdims=True), (8, 128))

    acc[...] = jnp.zeros_like(acc)

    def factors(k):
        fetch_tab(k, 0).start()
        fetch_tab(k, 0).wait()
        fac[...] = jnp.dot(onehot[...], tabs[0], preferred_element_type=F32)

    @pl.loop(0, STEPS)
    def _(k):
        lanes = pl.ds(pl.multiple_of(k * STEP, STEP), STEP)
        factors(k)

        @pl.loop(0, TEMPLATES // 16)
        def _(b):
            for tile in range(2):
                r = 4 * k + 2 * tile
                re = wide[pl.ds(b * 16 * ROWS + r, 16, stride=ROWS), :]
                im = wide[pl.ds(b * 16 * ROWS + r + 1, 16, stride=ROWS), :]
                for j in range(SHIFTS):
                    rows = pl.ds(pl.multiple_of(j * 128 + b * 16, 16), 16)
                    c = fac[rows, tile * 256:tile * 256 + 128]
                    s = fac[rows, tile * 256 + 128:tile * 256 + 256]
                    rot[rows, tile * 256:tile * 256 + 128] = (re * c + im * s).astype(BF16)
                    rot[rows, tile * 256 + 128:tile * 256 + 256] = (im * c - re * s).astype(BF16)

        acc[...] += lax.dot_general(rot[...], x[:, lanes], (((1,), (1,)), ((), ())),
                                    preferred_element_type=F32)

    precision = prec[...]

    def score(i, top):
        rows = pl.ds(pl.multiple_of(i * 8, 8), 8)
        half = norm[pl.ds(pl.multiple_of((i % 16) * 8, 8), 8), :]
        value = precision * (acc[rows, :] - jnp.concatenate([half] * 4, axis=1))
        acc[rows, :] = value
        return jnp.maximum(top, value)

    top = lax.fori_loop(0, PAIRS // 8, score, jnp.full((8, N_IMG), -jnp.inf, F32), unroll=4)
    top = jnp.max(top, axis=0, keepdims=True)

    def exponent(i, total):
        rows = pl.ds(pl.multiple_of(i * 8, 8), 8)
        value = jnp.exp(acc[rows, :] - top)
        acc[rows, :] = value
        return total + value

    total = lax.fori_loop(0, PAIRS // 8, exponent, jnp.zeros((8, N_IMG), F32), unroll=4)
    scale = 1.0 / jnp.sum(total, axis=0, keepdims=True)

    @pl.loop(0, TEMPLATES // 16)
    def _(b):
        total = jnp.zeros((16, 128), F32)
        for j in range(SHIFTS):
            rows = pl.ds(pl.multiple_of(j * 128 + b * 16, 16), 16)
            weight = (acc[rows, :] * scale).astype(BF16)
            wt[rows, :] = weight
            weight = weight.astype(F32)
            for lanes in range(4):
                total += weight[:, lanes * 128:lanes * 128 + 128]
        p_ref[pl.ds(b * 16 * ROWS_ALL + ROWS, 16, stride=ROWS_ALL), :] = total
        for r in range(ROWS + 1, ROWS_ALL):
            p_ref[pl.ds(b * 16 * ROWS_ALL + r, 16, stride=ROWS_ALL), :] = jnp.zeros((16, 128), F32)

    @pl.loop(0, STEPS)
    def _(k):
        lanes = pl.ds(pl.multiple_of(k * STEP, STEP), STEP)
        factors(k)
        acc[...] = jnp.dot(wt[...], x[:, lanes], preferred_element_type=F32)

        @pl.loop(0, TEMPLATES // 8)
        def _(b):
            for tile in range(2):
                back_re = jnp.zeros((8, 128), F32)
                back_im = jnp.zeros((8, 128), F32)
                for j in range(SHIFTS):
                    rows = pl.ds(pl.multiple_of(j * 128 + b * 8, 8), 8)
                    c = fac[rows, tile * 256:tile * 256 + 128]
                    s = fac[rows, tile * 256 + 128:tile * 256 + 256]
                    re = acc[rows, tile * 256:tile * 256 + 128]
                    im = acc[rows, tile * 256 + 128:tile * 256 + 256]
                    back_re += re * c - im * s
                    back_im += im * c + re * s
                r = 4 * k + 2 * tile
                p_ref[pl.ds(b * 8 * ROWS_ALL + r, 8, stride=ROWS_ALL), :] = back_re
                p_ref[pl.ds(b * 8 * ROWS_ALL + r + 1, 8, stride=ROWS_ALL), :] = back_im


def body(images, precision, templates, template_id, shift_table):
    vmem = pl.BlockSpec(memory_space=pltpu.VMEM)
    anywhere = pl.BlockSpec(memory_space=pl.ANY)
    dma = pltpu.SemaphoreType.DMA
    img = images.reshape(N_IMG, 2, 32, 128).transpose(0, 2, 1, 3).reshape(N_IMG * ROWS, 128)
    own = templates.reshape(2, 32, 128).transpose(1, 0, 2).reshape(ROWS, 128)
    tab = jnp.asarray(phase_constant())
    gathered = pl.pallas_call(
        gather_kernel,
        out_shape=jax.ShapeDtypeStruct((2, 4, 4, 4, ROWS, 128), BF16),
        in_specs=[vmem], out_specs=vmem,
        scratch_shapes=[dma((4, 4, 3)), dma((4, 4, 3))],
        compiler_params=pltpu.CompilerParams(collective_id=0, has_side_effects=True,
                                             vmem_limit_bytes=16 * MIB),
        name="gather",
    )(own)
    part = pl.pallas_call(
        compute_kernel,
        out_shape=jax.ShapeDtypeStruct((TEMPLATES * ROWS_ALL, 128), F32),
        in_specs=[anywhere, anywhere, vmem, vmem, vmem, vmem], out_specs=vmem,
        scratch_shapes=[
            pltpu.VMEM((N_IMG, 2 * COEFFS), BF16),
            pltpu.VMEM((2, 4096, 128), BF16),
            pltpu.VMEM((TEMPLATES * ROWS, 128), F32),
            pltpu.VMEM((PAIRS, STEP), F32),
            pltpu.VMEM((PAIRS, N_IMG), F32),
            pltpu.VMEM((PAIRS, STEP), BF16),
            pltpu.VMEM((PAIRS, N_IMG), BF16),
            pltpu.VMEM((PAIRS, 192), BF16),
            pltpu.VMEM((TEMPLATES, 128), F32),
            pltpu.VMEM((2, 192, STEP), BF16),
            dma((2,)), dma((2,)),
        ],
        compiler_params=pltpu.CompilerParams(vmem_limit_bytes=56 * MIB),
        name="compute",
    )(img, tab, gathered.reshape(TEMPLATES, ROWS, 128), precision.reshape(1, N_IMG),
      template_id.reshape(1, TEMPLATES), shift_table.T)
    out = pl.pallas_call(
        scatter_kernel,
        out_shape=jax.ShapeDtypeStruct((ROWS, 128), F32),
        in_specs=[anywhere, vmem], out_specs=vmem,
        scratch_shapes=[
            pltpu.VMEM((2, 4, 4, 4, ROWS_ALL, 128), F32),
            pltpu.VMEM((4, 4, 4, ROWS_ALL, 128), F32),
            pltpu.VMEM((3, 4, 4, ROWS_ALL, 128), F32),
            pltpu.VMEM((3, 4, ROWS_ALL, 128), F32),
            pltpu.VMEM((3, ROWS_ALL, 128), F32),
            dma((9, 4, 3)), dma((9, 4, 3)), dma,
        ],
        compiler_params=pltpu.CompilerParams(collective_id=1, has_side_effects=True,
                                             vmem_limit_bytes=24 * MIB),
        name="scatter",
    )(part.reshape(2, 4, 4, 4, ROWS_ALL, 128), own)
    return out.reshape(32, 2, 128).transpose(1, 0, 2).reshape(1, 2, COEFFS)


def solution(mesh):
    return jax.shard_map(
        body,
        mesh=mesh,
        in_specs=(
            P(("row", "col"), None, None),
            P(("row", "col")),
            P(("row", "col"), None, None),
            P(),
            P(),
        ),
        out_specs=P(("row", "col"), None, None),
        check_vma=False,
    )
```

time: 488 us -> 167 us (0.34)
  waiting for transfers between devices: 234 us -> 0 us
  Pallas kernels: 0 us -> 160 us
  other arithmetic: 79.6 us -> 0 us
  blocking collectives: 63 us -> 0 us
  local copies, waits for them, and re-layouts: 57.6 us -> 5.03 us
  matrix products: 33.4 us -> 0 us
  between operations: 14.5 us -> 0.05 us
    pallas_call x0 -> x3, Pallas kernels: none -> 160 us  [the longest x1 114 us: body(): pl.pallas_call(compute_kernel, out_shape=jax.ShapeDtypeStruct((TEMPLATES...]
    all_gather x1 -> x0, waiting for transfers between devices: 145 us -> none  [body(): pieces = lax.all_gather(templates, ('row', 'col'), axis=0, tiled=True)]
    unnamed x3 -> x0, waiting for transfers between devices: 89.2 us -> none
    psum x1 -> x0, blocking collectives: 63 us -> none  [body(): all_totals = lax.psum(weight_sums, ('row', 'col'))]
    reduce_sum x5 -> x0, other arithmetic: 43.8 us -> none  [the longest x1 40.8 us: body(): jnp.sum(back_real, axis=1)]
    dot_general x2 -> x0, matrix products: 33.4 us -> none  [the longest x1 18.9 us: body(): lax.dot_general(weights, flat_images, (((0,), (0,)), ((), ())), preferred...]
    another operation x3 -> x0, other arithmetic: 26.8 us -> none
    gather x4 -> x0, local copies, waits for them, and re-layouts: 20.6 us -> none  [the longest x2 18.7 us: shift_parts(): return (cos_table[shift_rows], sin_table[shift_rows])]
  transfers between devices with their start and end apart: 2 -> 0, of which waited for: 2 -> 0; matrix products, arithmetic and copies ran while one was open for 11% -> 0% of each run, Pallas kernels for 0% -> 0%
where the time goes in v1:
time: 167 us; the launch traced here: 166 us
  Pallas kernels  160 us (96%)
  local copies, waits for them, and re-layouts  5.03 us (3%)
    pallas_call x1, Pallas kernels, body(): pl.pallas_call(compute_kernel, out_shape=jax.ShapeDtypeStruct((TEMPLATES...  114 us
    pallas_call x1, Pallas kernels, body(): pl.pallas_call(scatter_kernel, out_shape=jax.ShapeDtypeStruct((ROWS, 128)...  25.2 us
    pallas_call x1, Pallas kernels, body(): pl.pallas_call(gather_kernel, out_shape=jax.ShapeDtypeStruct((2, 4, 4, 4,...  21.7 us
    unnamed x9, local copies, waits for them, and re-layouts  5.03 us

profile of v1, /device:TPU:0, one launch (start us, length us, event | category | flops | bytes accessed | tf_op | source)
XLA Modules:
  0.0 165.6 jit_solution(14202361464203411008)
XLA Ops:
  0.0 0.0 copy-start.2
  0.0 0.7 copy-done.2
  0.7 21.7 %gather.1 = bf16[2,4,4,4,64,128]{5,4,3,2,1,0:T(8,128)(2,1)S(1)} custom-call(bf16[64,128]{1,0:T(8,128)(2,1)S(1)} %bitcast.23), custom_call_target="tpu_custom_call" | custom-call | tf_op jit(solution)/shard_map/gather/pallas_call | solution.py:330
  22.4 0.0 copy-start.1
  22.4 1.4 copy-done.1
  23.8 0.0 copy-start.3
  23.8 113.6 %compute.1 = f32[9216,128]{1,0:T(8,128)} custom-call(bf16[32768,128]{1,0:T(8,128)(2,1)} %bitcast.25, bf16[192,8192]{1,0:T(8,128)(2,1)} %constant.2.clone.tab, bf16[128,64,128]{2,1,0:T(8,128)(2,1)} %bitcast.21, f32[1,512]{1,0:T(1,128)} %bitcast.27, s32[1,128]{1,0:T(1,128)} %bitcast.28, s32[8,128]{1,0:T(8,128)} %bitcast.26), custom_call_target="tpu_custom_call" | custom-call | tf_op jit(solution)/shard_map/compute/pallas_call | solution.py:339
  137.4 0.0 copy-done.3
  137.4 0.0 copy-start
  137.4 2.3 %copy-done = f32[9216,128]{1,0:T(8,128)S(1)} copy-done((f32[9216,128]{1,0:T(8,128)S(1)}, f32[9216,128]{1,0:T(8,128)}, u32[]{:S(2)}) %copy-start) | copy-done | bytes 4718616
  139.7 25.2 %scatter.1 = f32[64,128]{1,0:T(8,128)S(1)} custom-call(f32[2,4,4,4,72,128]{5,4,3,2,1,0:T(8,128)S(1)} %bitcast.20, bf16[64,128]{1,0:T(8,128)(2,1)S(1)} %bitcast.24), custom_call_target="tpu_custom_call" | custom-call | tf_op jit(solution)/shard_map/scatter/pallas_call | solution.py:360
  164.9 0.6 copy.11
Async XLA Ops:
  0.0 0.7 copy-start.2
  22.4 1.4 copy-start.1
  23.8 113.6 %copy-start.3 = (bf16[1,2,4096]{2,1,0:T(2,128)(2,1)S(1)}, bf16[1,2,4096]{2,1,0:T(2,128)(2,1)}, u32[]{:S(2)}) copy-start(bf16[1,2,4096]{2,1,0:T(2,128)(2,1)} %param.8) | copy-start | bytes 49156
  137.4 2.3 %copy-start = (f32[9216,128]{1,0:T(8,128)S(1)}, f32[9216,128]{1,0:T(8,128)}, u32[]{:S(2)}) copy-start(f32[9216,128]{1,0:T(8,128)} %compute.1) | copy-start | bytes 14155780

commit v2 on v1

v2 whole, which is shorter than its diff:
```python
import functools

import jax
import jax.numpy as jnp
import ml_dtypes
import numpy as np
from jax import lax
from jax.experimental import pallas as pl
from jax.experimental.pallas import tpu as pltpu
from jax.sharding import PartitionSpec as P

MESH = pl.DeviceIdType.MESH
F32 = jnp.float32
BF16 = jnp.bfloat16

GRID = 64
COEFFS = 4096
TEMPLATES = 128
SHIFTS = 8
PAIRS = TEMPLATES * SHIFTS
N_IMG = 512
ROWS = 64
STEP = 512
STEPS = 2 * COEFFS // STEP
HALF_STEPS = STEPS // 2
CHUNKS = 9
PRIOR_WEIGHT = 4.0
RB, BB = 32, 16
MIB = 1 << 20

ORDERS = ((2, 1, 0), (1, 0, 2), (0, 2, 1))


def phase_constant():
    c = np.arange(COEFFS)
    fx = c // GRID - GRID // 2
    fy = c % GRID - GRID // 2
    s = np.arange(64)
    k = ((s // 8 - 4)[:, None] * fx[None] + (s % 8 - 4)[:, None] * fy[None]) % GRID
    angle = k * (2.0 * np.pi / GRID)
    both = np.stack([np.cos(angle), np.sin(angle)], 1).reshape(64, 2, 32, 128)
    both = both.transpose(0, 2, 1, 3).reshape(64, 2 * COEFFS)[:, :COEFFS].astype(np.float32)
    high = both.astype(ml_dtypes.bfloat16)
    rest = both - high.astype(np.float32)
    mid = rest.astype(ml_dtypes.bfloat16)
    low = (rest - mid.astype(np.float32)).astype(ml_dtypes.bfloat16)
    return np.concatenate([high, mid, low], 0)


def place():
    row, col = lax.axis_index("row"), lax.axis_index("col")
    z, y_lo = row % 4, row // 4
    core, x, y_hi = col % 2, (col // 2) % 4, col // 8
    return core, (z, y_hi * 2 + y_lo, x)


def device(core, at):
    z, y, x = at
    return ((y % 2) * 4 + z, ((y // 2) * 4 + x) * 2 + core)


def moved(at, axis, by):
    return tuple((v + by) % 4 if i == axis else v for i, v in enumerate(at))


def enter(core, at):
    barrier = pltpu.get_barrier_semaphore()
    others = [device(1 - core, at)]
    others += [device(core, moved(at, a, d)) for a in range(3) for d in (1, 2, 3)]
    for other in others:
        pl.semaphore_signal(barrier, inc=1, device_id=other, device_id_type=MESH)
    pl.semaphore_wait(barrier, len(others))


def em_kernel(img, tab, own_t, prec, tid, table, out_ref,
              x, raw, wide, fac, acc, rot_a, rot_b, buf_a, buf_b, wts, onehot, sign, norm, tabs,
              got, part, r0, mine, r1, r2, r3, final,
              img_sem, tab_sem, gs_sem, gr_sem, ss_sem, sr_sem):
    core, at = place()

    groups = [(pl.ds(16 * g, 16), (ORDERS + ORDERS)[g]) for g in range(4)]

    def view(rows, order, stage, where):
        done = order[:stage]
        index = tuple(slice(None) if a in done else where[a] for a in range(3))
        return got.at[(core,) + index + (rows,)]

    def g_copy(g, stage, d, arrived=False):
        rows, order = groups[g]
        if stage == 3:
            ref = got.at[1 - core if arrived else core, :, :, :, rows]
            target = device(1 - core, at)
        else:
            axis = order[stage]
            ref = view(rows, order, stage, moved(at, axis, 4 - d) if arrived else at)
            target = device(core, moved(at, axis, d))
        return pltpu.make_async_remote_copy(
            src_ref=ref, dst_ref=ref, send_sem=gs_sem.at[g, stage, d - 1],
            recv_sem=gr_sem.at[g, stage, d - 1], device_id=target, device_id_type=MESH)

    def g_each(stage):
        return (1, 3, 2) if stage < 3 else (1,)

    def g_stage(stage):
        for g in range(4):
            if stage:
                for d in g_each(stage - 1):
                    g_copy(g, stage - 1, d, True).wait_recv()
            if stage < 4:
                for d in g_each(stage):
                    g_copy(g, stage, d).start()

    lands = (r0, r1, r2, r3)

    def s_copy(c, o, stage, d):
        order = ORDERS[o]
        if stage == 0:
            src = part.at[pl.ds(pl.multiple_of(c * 1024 + (1 - core) * 512, 512), 512)]
            dst = r0.at[c]
            target = device(1 - core, at)
        else:
            axis = order[stage - 1]
            other = moved(at, axis, d)
            index = [at[a] if a in order[:stage - 1] else slice(None) for a in range(3)]
            index[axis] = other[axis]
            src = mine.at[(c,) + tuple(index)]
            dst = lands[stage].at[c, d - 1]
            target = device(core, other)
        return pltpu.make_async_remote_copy(
            src_ref=src, dst_ref=dst, send_sem=ss_sem.at[c, stage, d - 1],
            recv_sem=sr_sem.at[c, stage, d - 1], device_id=target, device_id_type=MESH)

    def s_each(stage):
        return (1, 3, 2) if stage else (1,)

    def s_take(c, o, stage):
        for d in s_each(stage):
            s_copy(c, o, stage, d).wait_recv()
        if stage == 0:
            total = part[pl.ds(pl.multiple_of(c * 1024 + core * 512, 512), 512), :] + r0[c]
            mine[c] = total.reshape(4, 4, 4, 8, 128)
            return
        index = (c,) + tuple(at[a] if a in ORDERS[o][:stage] else slice(None) for a in range(3))
        total = mine[index]
        for d in (1, 2, 3):
            total += lands[stage][c, d - 1]
        if stage == 3:
            final[pl.ds(pl.multiple_of(c * 8, 8), 8), :] = total
        else:
            mine[index] = total

    def s_advance(c, stage):
        for o in range(3):
            @pl.when(jnp.logical_and(jnp.logical_and(c >= 0, c < CHUNKS), c % 3 == o))
            def _():
                if stage:
                    s_take(c, o, stage - 1)
                if stage < 4:
                    for d in s_each(stage):
                        s_copy(c, o, stage, d).start()

    def fetch(b):
        return pltpu.make_async_copy(img.at[pl.ds(b * 4096, 4096)], raw.at[b % 2], img_sem.at[b % 2])

    def relayout(b):
        if b < 7:
            fetch(b + 1).start()
        fetch(b).wait()
        wide[pl.ds(0, 4096)] = raw[b % 2].astype(F32)

        @pl.loop(0, ROWS)
        def _(r):
            lanes = pl.ds(pl.multiple_of(r * 128, 128), 128)
            x[pl.ds(b * 64, 64), lanes] = wide[pl.ds(r, 64, stride=ROWS), :].astype(BF16)

    def choose():
        ids = lax.broadcasted_iota(jnp.int32, (128, 128), 0)
        pick = jnp.where(ids == tid[...], 1.0, 0.0).astype(BF16)
        shifts_t = jnp.dot(table[...].astype(F32).astype(BF16), pick, preferred_element_type=F32)
        slot = lax.broadcasted_iota(jnp.int32, (128, 128), 1)
        row, col = slot // 16, slot % 16
        inner = (col % 2) * 64 + (row % 4) * 16 + ((col // 8) * 2 + row // 4) * 4 + (col // 2) % 4
        perm = jnp.where(ids == inner, 1.0, 0.0).astype(BF16)
        shifts = lax.dot_general(perm, shifts_t.astype(BF16), (((1,), (1,)), ((), ())),
                                 preferred_element_type=F32)
        lane = lax.broadcasted_iota(jnp.int32, (128, 64), 1).astype(F32)
        odd_lane = jnp.where((lax.broadcasted_iota(jnp.int32, (128, 64), 1) // 8) % 2 == 1, 1.0, 0.0)
        for j in range(SHIFTS):
            one = jnp.where(lane == shifts[:, j:j + 1], 1.0, 0.0)
            odd = jnp.sum(one * odd_lane, axis=1, keepdims=True)
            sign[pl.ds(j * 128, 128), :] = jnp.broadcast_to(1.0 - 2.0 * odd, (128, 128))
            one = one.astype(BF16)
            onehot[pl.ds(j * 128, 128), :] = jnp.concatenate([one, one, one], axis=1)

    def widen(half):
        @pl.loop(0, 16)
        def _(i):
            for k in range(4):
                rows = pl.ds(pl.multiple_of((half * 64 + i * 4 + k) * ROWS, ROWS), ROWS)
                wide[rows] = got[half, i // 4, i % 4, k].astype(F32)

    tab_copy = pltpu.make_async_copy(tab, tabs, tab_sem)
    fetch(0).start()
    tab_copy.start()
    enter(core, at)
    got[core, at[0], at[1], at[2]] = own_t[...]
    g_stage(0)
    choose()
    norm[...] = jnp.zeros_like(norm)
    acc[...] = jnp.zeros_like(acc)
    relayout(0)
    relayout(1)
    g_stage(1)
    for b in (2, 3, 4):
        relayout(b)
    g_stage(2)
    for b in (5, 6, 7):
        relayout(b)
    g_stage(3)
    widen(core)
    tab_copy.wait()
    for k in range(4):
        lanes = slice(k * 1024, k * 1024 + 1024)
        fac[:, lanes] = jnp.dot(onehot[...], tabs[:, lanes], preferred_element_type=F32)
    g_stage(4)
    widen(1 - core)

    def factor(q, rows, tile):
        start = pl.multiple_of((q % HALF_STEPS) * STEP + tile * 256, 256)
        return fac[rows, pl.ds(start, 128)], fac[rows, pl.ds(start + 128, 128)]

    def rotate(q, rot):
        count = jnp.where(q < STEPS, 1.0, 0.0)
        for b in range(TEMPLATES // RB):
            squares = jnp.zeros((RB, 128), F32)
            for tile in range(2):
                r = b * RB * ROWS + ((q + HALF_STEPS) % STEPS) * 4 + 2 * tile
                re = wide[pl.ds(r, RB, stride=ROWS), :]
                im = wide[pl.ds(r + 1, RB, stride=ROWS), :]
                squares += re * re + im * im
                for j in range(SHIFTS):
                    rows = pl.ds(j * 128 + b * RB, RB)
                    c, s = factor(q, rows, tile)
                    rot[rows, tile * 256:tile * 256 + 128] = (re * c + im * s).astype(BF16)
                    rot[rows, tile * 256 + 128:tile * 256 + 256] = (im * c - re * s).astype(BF16)
            norm[b * RB:b * RB + RB, :] += squares * count

    def images(q):
        return x[:, pl.ds(pl.multiple_of((q % STEPS) * STEP, STEP), STEP)]

    def add_scores(q, rot):
        acc[...] += lax.dot_general(rot[...], images(q + HALF_STEPS), (((1,), (1,)), ((), ())),
                                    preferred_element_type=F32)

    def four(value):
        return jnp.concatenate([value] * 4, axis=1)

    rotate(0, rot_a)

    @pl.loop(0, 2)
    def _(half):
        @pl.loop(0, PAIRS // 32)
        def _(i):
            rows = pl.ds(pl.multiple_of(i * 32, 32), 32)
            acc[rows, :] *= four(sign[rows, :])

        @pl.loop(0, HALF_STEPS // 2)
        def _(i):
            q = half * HALF_STEPS + 2 * i
            add_scores(q, rot_a)
            rotate(q + 1, rot_b)
            add_scores(q + 1, rot_b)
            rotate(q + 2, rot_a)

    precision = prec[...]
    norm[...] = jnp.broadcast_to(0.5 * jnp.sum(norm[...], axis=1, keepdims=True), (TEMPLATES, 128))

    def score(i, top):
        rows = pl.ds(pl.multiple_of(i * 8, 8), 8)
        half = norm[pl.ds(pl.multiple_of((i % 16) * 8, 8), 8), :]
        value = precision * (acc[rows, :] - four(half))
        acc[rows, :] = value
        return jnp.maximum(top, value)

    top = lax.fori_loop(0, PAIRS // 8, score, jnp.full((8, N_IMG), -jnp.inf, F32), unroll=4)
    top = jnp.max(top, axis=0, keepdims=True)

    def exponent(i, total):
        rows = pl.ds(pl.multiple_of(i * 8, 8), 8)
        value = jnp.exp(acc[rows, :] - top)
        acc[rows, :] = value
        return total + value

    total = lax.fori_loop(0, PAIRS // 8, exponent, jnp.zeros((8, N_IMG), F32), unroll=4)
    scale = 1.0 / jnp.sum(total, axis=0, keepdims=True)

    @pl.loop(0, TEMPLATES // 16)
    def _(b):
        total = jnp.zeros((16, 128), F32)
        for j in range(SHIFTS):
            rows = pl.ds(pl.multiple_of(j * 128 + b * 16, 16), 16)
            weight = (acc[rows, :] * scale).astype(BF16)
            wts[0, rows, :] = weight
            weight = weight.astype(F32)
            wts[1, rows, :] = (weight * four(sign[rows, :])).astype(BF16)
            for lanes in range(4):
                total += weight[:, lanes * 128:lanes * 128 + 128]
        part[pl.ds(b * 128, 16, stride=8), :] = total
        for r in range(1, 8):
            part[pl.ds(b * 128 + r, 16, stride=8), :] = jnp.zeros((16, 128), F32)

    s_advance(jnp.int32(0), 0)

    def gather_images(q, buf):
        buf[...] = jnp.dot(wts[(q // HALF_STEPS) % 2], images(q), preferred_element_type=F32)

    def turn_back(q, buf, chunk, odd):
        for b in range(TEMPLATES // BB):
            for tile in range(2):
                back_re = jnp.zeros((BB, 128), F32)
                back_im = jnp.zeros((BB, 128), F32)
                for j in range(SHIFTS):
                    rows = pl.ds(j * 128 + b * BB, BB)
                    c, s = factor(q, rows, tile)
                    re = buf[rows, tile * 256:tile * 256 + 128]
                    im = buf[rows, tile * 256 + 128:tile * 256 + 256]
                    back_re += re * c - im * s
                    back_im += im * c + re * s
                r = chunk * 1024 + b * BB * 8 + odd * 4 + 2 * tile
                part[pl.ds(r, BB, stride=8), :] = back_re
                part[pl.ds(r + 1, BB, stride=8), :] = back_im

    gather_images(jnp.int32(0), buf_a)

    @pl.loop(0, STEPS // 2)
    def _(i):
        gather_images(2 * i + 1, buf_b)
        turn_back(2 * i, buf_a, i + 1, 0)
        gather_images(2 * i + 2, buf_a)
        turn_back(2 * i + 1, buf_b, i + 1, 1)
        for stage in range(5):
            s_advance(i + 1 - stage, stage)

    @pl.loop(CHUNKS, CHUNKS + 4)
    def _(i):
        for stage in range(1, 5):
            s_advance(i - stage, stage)

    @pl.loop(0, CHUNKS // 3)
    def _(i):
        for o in range(3):
            for stage in range(4):
                for d in s_each(stage):
                    s_copy(i * 3 + o, o, stage, d).wait_send()
    for stage in range(4):
        for g in range(4):
            for d in g_each(stage):
                g_copy(g, stage, d).wait_send()

    total = jnp.sum(final[0:8, :], keepdims=True) + PRIOR_WEIGHT
    out_ref[...] = (final[8:72, :] + PRIOR_WEIGHT * own_t[...].astype(F32)) / total


def body(images, precision, templates, template_id, shift_table):
    vmem = pl.BlockSpec(memory_space=pltpu.VMEM)
    anywhere = pl.BlockSpec(memory_space=pl.ANY)
    dma = pltpu.SemaphoreType.DMA
    img = images.reshape(N_IMG, 2, 32, 128).transpose(0, 2, 1, 3).reshape(N_IMG * ROWS, 128)
    own = templates.reshape(2, 32, 128).transpose(1, 0, 2).reshape(ROWS, 128)
    tab = jnp.asarray(phase_constant())
    out = pl.pallas_call(
        em_kernel,
        out_shape=jax.ShapeDtypeStruct((ROWS, 128), F32),
        in_specs=[anywhere, anywhere, vmem, vmem, vmem, vmem], out_specs=vmem,
        scratch_shapes=[
            pltpu.VMEM((N_IMG, 2 * COEFFS), BF16),
            pltpu.VMEM((2, 4096, 128), BF16),
            pltpu.VMEM((TEMPLATES * ROWS, 128), F32),
            pltpu.VMEM((PAIRS, COEFFS), F32),
            pltpu.VMEM((PAIRS, N_IMG), F32),
            pltpu.VMEM((PAIRS, STEP), BF16),
            pltpu.VMEM((PAIRS, STEP), BF16),
            pltpu.VMEM((PAIRS, STEP), F32),
            pltpu.VMEM((PAIRS, STEP), F32),
            pltpu.VMEM((2, PAIRS, N_IMG), BF16),
            pltpu.VMEM((PAIRS, 192), BF16),
            pltpu.VMEM((PAIRS, 128), F32),
            pltpu.VMEM((TEMPLATES, 128), F32),
            pltpu.VMEM((192, COEFFS), BF16),
            pltpu.VMEM((2, 4, 4, 4, ROWS, 128), BF16),
            pltpu.VMEM((CHUNKS * 1024, 128), F32),
            pltpu.VMEM((CHUNKS, 512, 128), F32),
            pltpu.VMEM((CHUNKS, 4, 4, 4, 8, 128), F32),
            pltpu.VMEM((CHUNKS, 3, 4, 4, 8, 128), F32),
            pltpu.VMEM((CHUNKS, 3, 4, 8, 128), F32),
            pltpu.VMEM((CHUNKS, 3, 8, 128), F32),
            pltpu.VMEM((72, 128), F32),
            dma((2,)), dma, dma((4, 4, 3)), dma((4, 4, 3)),
            dma((CHUNKS, 4, 3)), dma((CHUNKS, 4, 3)),
        ],
        compiler_params=pltpu.CompilerParams(collective_id=0, has_side_effects=True,
                                             vmem_limit_bytes=60 * MIB),
        name="em_step",
    )(img, tab, own, precision.reshape(1, N_IMG), template_id.reshape(1, TEMPLATES), shift_table.T)
    return out.reshape(32, 2, 128).transpose(1, 0, 2).reshape(1, 2, COEFFS)


def solution(mesh):
    return jax.shard_map(
        body,
        mesh=mesh,
        in_specs=(
            P(("row", "col"), None, None),
            P(("row", "col")),
            P(("row", "col"), None, None),
            P(),
            P(),
        ),
        out_specs=P(("row", "col"), None, None),
        check_vma=False,
    )
```

time: 167 us -> 97.1 us (0.58)
  Pallas kernels: 160 us -> 95.5 us
  local copies, waits for them, and re-layouts: 5.03 us -> 1.38 us
    pallas_call x3 -> x1, Pallas kernels: 160 us -> 95.5 us  [body(): pl.pallas_call(em_kernel, out_shape=jax.ShapeDtypeStruct((ROWS, 128), F32...]
    unnamed x9 -> x1, local copies, waits for them, and re-layouts: 5.03 us -> 1.38 us
where the time goes in v2:
time: 97.1 us; the launch traced here: 96.8 us
  Pallas kernels  95.5 us (98%)
  local copies, waits for them, and re-layouts  1.38 us (1%)
    pallas_call x1, Pallas kernels, body(): pl.pallas_call(em_kernel, out_shape=jax.ShapeDtypeStruct((ROWS, 128), F32...  95.5 us

profile of v2, /device:TPU:0, one launch (start us, length us, event | category | flops | bytes accessed | tf_op | source)
XLA Modules:
  0.0 96.8 jit_solution(10468233793532514855)
XLA Ops:
  0.0 95.5 %em_step.1 = f32[64,128]{1,0:T(8,128)} custom-call(bf16[32768,128]{1,0:T(8,128)(2,1)} %bitcast.18, bf16[192,4096]{1,0:T(8,128)(2,1)} %constant.2.clone.tab, bf16[64,128]{1,0:T(8,128)(2,1)} %bitcast.20, f32[1,512]{1,0:T(1,128)} %bitcast.22, s32[1,128]{1,0:T(1,128)} %bitcast.23, s32[8,128]{1,0:T(8,128)} %bitcast.21), custom_call_target="tpu_custom_call" | custom-call | tf_op jit(solution)/shard_map/em_step/pallas_call | solution.py:371
  95.5 1.4 %copy.11 = f32[1,2,4096]{2,1,0:T(2,128)} copy(f32[1,2,4096]{2,1,0:T(2,128)} %bitcast.19) | data formatting | bytes 65536

commit v3 on v2

--- a/solution.py
+++ b/solution.py
@@ -23,6 +23,8 @@
 STEP = 512
 STEPS = 2 * COEFFS // STEP
 HALF_STEPS = STEPS // 2
+PITCH = 65
+LAG = (0, 2, 6, 9, 11)
 CHUNKS = 9
 PRIOR_WEIGHT = 4.0
 RB, BB = 32, 16
@@ -166,12 +168,20 @@
         if b < 7:
             fetch(b + 1).start()
         fetch(b).wait()
-        wide[pl.ds(0, 4096)] = raw[b % 2].astype(F32)
-
-        @pl.loop(0, ROWS)
-        def _(r):
-            lanes = pl.ds(pl.multiple_of(r * 128, 128), 128)
-            x[pl.ds(b * 64, 64), lanes] = wide[pl.ds(r, 64, stride=ROWS), :].astype(BF16)
+
+        @pl.loop(0, 8)
+        def _(i):
+            for k in range(8):
+                n = i * 8 + k
+                rows = pl.ds(pl.multiple_of(n * ROWS, ROWS), ROWS)
+                wide[pl.ds(n * PITCH, ROWS)] = raw[b % 2, rows].astype(F32)
+
+        @pl.loop(0, ROWS // 8)
+        def _(i):
+            for k in range(8):
+                r = i * 8 + k
+                lanes = pl.ds(pl.multiple_of(r * 128, 128), 128)
+                x[pl.ds(b * 64, 64), lanes] = wide[pl.ds(r, 64, stride=PITCH), :].astype(BF16)
 
     def choose():
         ids = lax.broadcasted_iota(jnp.int32, (128, 128), 0)
@@ -196,7 +206,7 @@
         @pl.loop(0, 16)
         def _(i):
             for k in range(4):
-                rows = pl.ds(pl.multiple_of((half * 64 + i * 4 + k) * ROWS, ROWS), ROWS)
+                rows = pl.ds((half * 64 + i * 4 + k) * PITCH, ROWS)
                 wide[rows] = got[half, i // 4, i % 4, k].astype(F32)
 
     tab_copy = pltpu.make_async_copy(tab, tabs, tab_sem)
@@ -234,9 +244,9 @@
         for b in range(TEMPLATES // RB):
             squares = jnp.zeros((RB, 128), F32)
             for tile in range(2):
-                r = b * RB * ROWS + ((q + HALF_STEPS) % STEPS) * 4 + 2 * tile
-                re = wide[pl.ds(r, RB, stride=ROWS), :]
-                im = wide[pl.ds(r + 1, RB, stride=ROWS), :]
+                r = b * RB * PITCH + ((q + HALF_STEPS) % STEPS) * 4 + 2 * tile
+                re = wide[pl.ds(r, RB, stride=PITCH), :]
+                im = wide[pl.ds(r + 1, RB, stride=PITCH), :]
                 squares += re * re + im * im
                 for j in range(SHIFTS):
                     rows = pl.ds(j * 128 + b * RB, RB)
@@ -339,12 +349,12 @@
         gather_images(2 * i + 2, buf_a)
         turn_back(2 * i + 1, buf_b, i + 1, 1)
         for stage in range(5):
-            s_advance(i + 1 - stage, stage)
-
-    @pl.loop(CHUNKS, CHUNKS + 4)
+            s_advance(i + 1 - LAG[stage], stage)
+
+    @pl.loop(CHUNKS, CHUNKS + LAG[4])
     def _(i):
         for stage in range(1, 5):
-            s_advance(i - stage, stage)
+            s_advance(i - LAG[stage], stage)
 
     @pl.loop(0, CHUNKS // 3)
     def _(i):
@@ -375,7 +385,7 @@
         scratch_shapes=[
             pltpu.VMEM((N_IMG, 2 * COEFFS), BF16),
             pltpu.VMEM((2, 4096, 128), BF16),
-            pltpu.VMEM((TEMPLATES * ROWS, 128), F32),
+            pltpu.VMEM((TEMPLATES * PITCH, 128), F32),
             pltpu.VMEM((PAIRS, COEFFS), F32),
             pltpu.VMEM((PAIRS, N_IMG), F32),
             pltpu.VMEM((PAIRS, STEP), BF16),

time: 97.1 us -> 75 us (0.77)
  Pallas kernels: 95.5 us -> 73.3 us
    pallas_call x1, Pallas kernels: 95.5 us -> 73.3 us  [body(): pl.pallas_call(em_kernel, out_shape=jax.ShapeDtypeStruct((ROWS, 128), F32...]
where the time goes in v3:
time: 75 us; the launch traced here: 74.7 us
  Pallas kernels  73.3 us (98%)
  local copies, waits for them, and re-layouts  1.38 us (2%)
    pallas_call x1, Pallas kernels, body(): pl.pallas_call(em_kernel, out_shape=jax.ShapeDtypeStruct((ROWS, 128), F32...  73.3 us

profile of v3, /device:TPU:0, one launch (start us, length us, event | category | flops | bytes accessed | tf_op | source)
XLA Modules:
  0.0 74.7 jit_solution(13532879893957887667)
XLA Ops:
  0.0 73.3 %em_step.1 = f32[64,128]{1,0:T(8,128)} custom-call(bf16[32768,128]{1,0:T(8,128)(2,1)} %bitcast.18, bf16[192,4096]{1,0:T(8,128)(2,1)} %constant.2.clone.tab, bf16[64,128]{1,0:T(8,128)(2,1)} %bitcast.20, f32[1,512]{1,0:T(1,128)} %bitcast.22, s32[1,128]{1,0:T(1,128)} %bitcast.23, s32[8,128]{1,0:T(8,128)} %bitcast.21), custom_call_target="tpu_custom_call" | custom-call | tf_op jit(solution)/shard_map/em_step/pallas_call | solution.py:381
  73.3 1.4 %copy.11 = f32[1,2,4096]{2,1,0:T(2,128)} copy(f32[1,2,4096]{2,1,0:T(2,128)} %bitcast.19) | data formatting | bytes 65536

commit v4 on v3

--- a/solution.py
+++ b/solution.py
@@ -24,7 +24,7 @@
 STEPS = 2 * COEFFS // STEP
 HALF_STEPS = STEPS // 2
 PITCH = 65
-LAG = (0, 2, 6, 9, 11)
+LAG = (0, 2, 7, 11, 13)
 CHUNKS = 9
 PRIOR_WEIGHT = 4.0
 RB, BB = 32, 16
@@ -87,18 +87,20 @@
         index = tuple(slice(None) if a in done else where[a] for a in range(3))
         return got.at[(core,) + index + (rows,)]
 
-    def g_copy(g, stage, d, arrived=False):
+    def g_copy(g, stage, d):
         rows, order = groups[g]
         if stage == 3:
-            ref = got.at[1 - core if arrived else core, :, :, :, rows]
+            ref = got.at[core, :, :, :, rows]
             target = device(1 - core, at)
         else:
-            axis = order[stage]
-            ref = view(rows, order, stage, moved(at, axis, 4 - d) if arrived else at)
-            target = device(core, moved(at, axis, d))
+            ref = view(rows, order, stage, at)
+            target = device(core, moved(at, order[stage], d))
         return pltpu.make_async_remote_copy(
-            src_ref=ref, dst_ref=ref, send_sem=gs_sem.at[g, stage, d - 1],
-            recv_sem=gr_sem.at[g, stage, d - 1], device_id=target, device_id_type=MESH)
+            src_ref=ref, dst_ref=ref, send_sem=gs_sem, recv_sem=gr_sem.at[g, stage],
+            device_id=target, device_id_type=MESH)
+
+    def await_bytes(ref, sem):
+        pltpu.make_async_copy(ref, ref, sem).wait()
 
     def g_each(stage):
         return (1, 3, 2) if stage < 3 else (1,)
@@ -106,8 +108,7 @@
     def g_stage(stage):
         for g in range(4):
             if stage:
-                for d in g_each(stage - 1):
-                    g_copy(g, stage - 1, d, True).wait_recv()
+                await_bytes(raw.at[0, pl.ds(0, 16 * (3, 12, 48, 64)[stage - 1])], gr_sem.at[g, stage - 1])
             if stage < 4:
                 for d in g_each(stage):
                     g_copy(g, stage, d).start()
@@ -129,15 +130,14 @@
             dst = lands[stage].at[c, d - 1]
             target = device(core, other)
         return pltpu.make_async_remote_copy(
-            src_ref=src, dst_ref=dst, send_sem=ss_sem.at[c, stage, d - 1],
-            recv_sem=sr_sem.at[c, stage, d - 1], device_id=target, device_id_type=MESH)
+            src_ref=src, dst_ref=dst, send_sem=ss_sem,
+            recv_sem=sr_sem.at[c, stage], device_id=target, device_id_type=MESH)
 
     def s_each(stage):
         return (1, 3, 2) if stage else (1,)
 
     def s_take(c, o, stage):
-        for d in s_each(stage):
-            s_copy(c, o, stage, d).wait_recv()
+        await_bytes(lands[stage].at[c], sr_sem.at[c, stage])
         if stage == 0:
             total = part[pl.ds(pl.multiple_of(c * 1024 + core * 512, 512), 512), :] + r0[c]
             mine[c] = total.reshape(4, 4, 4, 8, 128)
@@ -152,14 +152,16 @@
             mine[index] = total
 
     def s_advance(c, stage):
-        for o in range(3):
-            @pl.when(jnp.logical_and(jnp.logical_and(c >= 0, c < CHUNKS), c % 3 == o))
-            def _():
-                if stage:
-                    s_take(c, o, stage - 1)
-                if stage < 4:
-                    for d in s_each(stage):
-                        s_copy(c, o, stage, d).start()
+        @pl.when(jnp.logical_and(c >= 0, c < CHUNKS))
+        def _():
+            for o in range(3):
+                @pl.when(c % 3 == o)
+                def _():
+                    if stage:
+                        s_take(c, o, stage - 1)
+                    if stage < 4:
+                        for d in s_each(stage):
+                            s_copy(c, o, stage, d).start()
 
     def fetch(b):
         return pltpu.make_async_copy(img.at[pl.ds(b * 4096, 4096)], raw.at[b % 2], img_sem.at[b % 2])
@@ -356,16 +358,8 @@
         for stage in range(1, 5):
             s_advance(i - LAG[stage], stage)
 
-    @pl.loop(0, CHUNKS // 3)
-    def _(i):
-        for o in range(3):
-            for stage in range(4):
-                for d in s_each(stage):
-                    s_copy(i * 3 + o, o, stage, d).wait_send()
-    for stage in range(4):
-        for g in range(4):
-            for d in g_each(stage):
-                g_copy(g, stage, d).wait_send()
+    await_bytes(part.at[pl.ds(0, CHUNKS * (512 + 504))], ss_sem)
+    await_bytes(wide.at[pl.ds(0, 32 * 127)], gs_sem)
 
     total = jnp.sum(final[0:8, :], keepdims=True) + PRIOR_WEIGHT
     out_ref[...] = (final[8:72, :] + PRIOR_WEIGHT * own_t[...].astype(F32)) / total
@@ -405,8 +399,8 @@
             pltpu.VMEM((CHUNKS, 3, 4, 8, 128), F32),
             pltpu.VMEM((CHUNKS, 3, 8, 128), F32),
             pltpu.VMEM((72, 128), F32),
-            dma((2,)), dma, dma((4, 4, 3)), dma((4, 4, 3)),
-            dma((CHUNKS, 4, 3)), dma((CHUNKS, 4, 3)),
+            dma((2,)), dma, dma, dma((4, 4)),
+            dma, dma((CHUNKS, 4)),
         ],
         compiler_params=pltpu.CompilerParams(collective_id=0, has_side_effects=True,
                                              vmem_limit_bytes=60 * MIB),

time: 75 us -> 71.8 us (0.957)
  Pallas kernels: 73.3 us -> 70.1 us
    pallas_call x1, Pallas kernels: 73.3 us -> 70.1 us  [body(): pl.pallas_call(em_kernel, out_shape=jax.ShapeDtypeStruct((ROWS, 128), F32...]
where the time goes in v4:
time: 71.8 us; the launch traced here: 71.5 us
  Pallas kernels  70.1 us (98%)
  local copies, waits for them, and re-layouts  1.38 us (2%)
    pallas_call x1, Pallas kernels, body(): pl.pallas_call(em_kernel, out_shape=jax.ShapeDtypeStruct((ROWS, 128), F32...  70.1 us

profile of v4, /device:TPU:0, one launch (start us, length us, event | category | flops | bytes accessed | tf_op | source)
XLA Modules:
  0.0 71.5 jit_solution(15282368809494714221)
XLA Ops:
  0.0 70.1 %em_step.1 = f32[64,128]{1,0:T(8,128)} custom-call(bf16[32768,128]{1,0:T(8,128)(2,1)} %bitcast.18, bf16[192,4096]{1,0:T(8,128)(2,1)} %constant.2.clone.tab, bf16[64,128]{1,0:T(8,128)(2,1)} %bitcast.20, f32[1,512]{1,0:T(1,128)} %bitcast.22, s32[1,128]{1,0:T(1,128)} %bitcast.23, s32[8,128]{1,0:T(8,128)} %bitcast.21), custom_call_target="tpu_custom_call" | custom-call | tf_op jit(solution)/shard_map/em_step/pallas_call | solution.py:375
  70.1 1.4 %copy.11 = f32[1,2,4096]{2,1,0:T(2,128)} copy(f32[1,2,4096]{2,1,0:T(2,128)} %bitcast.19) | data formatting | bytes 65536

commit v5 on v4

--- a/solution.py
+++ b/solution.py
@@ -24,7 +24,7 @@
 STEPS = 2 * COEFFS // STEP
 HALF_STEPS = STEPS // 2
 PITCH = 65
-LAG = (0, 2, 7, 11, 13)
+LAG = (0, 2, 7, 15, 23)
 CHUNKS = 9
 PRIOR_WEIGHT = 4.0
 RB, BB = 32, 16
@@ -80,15 +80,15 @@
               img_sem, tab_sem, gs_sem, gr_sem, ss_sem, sr_sem):
     core, at = place()
 
-    groups = [(pl.ds(16 * g, 16), (ORDERS + ORDERS)[g]) for g in range(4)]
+    groups = [pl.ds(16 * g, 16) for g in range(4)]
 
     def view(rows, order, stage, where):
         done = order[:stage]
         index = tuple(slice(None) if a in done else where[a] for a in range(3))
         return got.at[(core,) + index + (rows,)]
 
-    def g_copy(g, stage, d):
-        rows, order = groups[g]
+    def g_copy(g, stage, d, order):
+        rows = groups[g]
         if stage == 3:
             ref = got.at[core, :, :, :, rows]
             target = device(1 - core, at)
@@ -109,9 +109,15 @@
         for g in range(4):
             if stage:
                 await_bytes(raw.at[0, pl.ds(0, 16 * (3, 12, 48, 64)[stage - 1])], gr_sem.at[g, stage - 1])
-            if stage < 4:
+            if stage < 4 and g < 3:
                 for d in g_each(stage):
-                    g_copy(g, stage, d).start()
+                    g_copy(g, stage, d, ORDERS[g]).start()
+            elif stage < 4:
+                for o in (0, 2):
+                    @pl.when(core * 2 == o)
+                    def _():
+                        for d in g_each(stage):
+                            g_copy(g, stage, d, ORDERS[o]).start()
 
     lands = (r0, r1, r2, r3)
 

time: 71.8 us -> 69.3 us (0.965)
  Pallas kernels: 70.1 us -> 67.6 us
    pallas_call x1, Pallas kernels: 70.1 us -> 67.6 us  [body(): pl.pallas_call(em_kernel, out_shape=jax.ShapeDtypeStruct((ROWS, 128), F32...]
where the time goes in v5:
time: 69.3 us; the launch traced here: 69 us
  Pallas kernels  67.6 us (98%)
  local copies, waits for them, and re-layouts  1.38 us (2%)
    pallas_call x1, Pallas kernels, body(): pl.pallas_call(em_kernel, out_shape=jax.ShapeDtypeStruct((ROWS, 128), F32...  67.6 us

profile of v5, /device:TPU:0, one launch (start us, length us, event | category | flops | bytes accessed | tf_op | source)
XLA Modules:
  0.0 69.0 jit_solution(16746144667878856495)
XLA Ops:
  0.0 67.6 %em_step.1 = f32[64,128]{1,0:T(8,128)} custom-call(bf16[32768,128]{1,0:T(8,128)(2,1)} %bitcast.18, bf16[192,4096]{1,0:T(8,128)(2,1)} %constant.2.clone.tab, bf16[64,128]{1,0:T(8,128)(2,1)} %bitcast.20, f32[1,512]{1,0:T(1,128)} %bitcast.22, s32[1,128]{1,0:T(1,128)} %bitcast.23, s32[8,128]{1,0:T(8,128)} %bitcast.21), custom_call_target="tpu_custom_call" | custom-call | tf_op jit(solution)/shard_map/em_step/pallas_call | solution.py:381
  67.6 1.4 %copy.11 = f32[1,2,4096]{2,1,0:T(2,128)} copy(f32[1,2,4096]{2,1,0:T(2,128)} %bitcast.19) | data formatting | bytes 65536

commit v6 on v5

--- a/solution.py
+++ b/solution.py
@@ -227,12 +227,11 @@
     norm[...] = jnp.zeros_like(norm)
     acc[...] = jnp.zeros_like(acc)
     relayout(0)
+    g_stage(1)
     relayout(1)
-    g_stage(1)
-    for b in (2, 3, 4):
-        relayout(b)
+    relayout(2)
     g_stage(2)
-    for b in (5, 6, 7):
+    for b in range(3, 8):
         relayout(b)
     g_stage(3)
     widen(core)

time: 69.3 us -> 69.3 us (level)
  no operation moved by 1% of the time
where the time goes in v6:
time: 69.3 us; the launch traced here: 68.9 us
  Pallas kernels  67.6 us (98%)
  local copies, waits for them, and re-layouts  1.38 us (2%)
    pallas_call x1, Pallas kernels, body(): pl.pallas_call(em_kernel, out_shape=jax.ShapeDtypeStruct((ROWS, 128), F32...  67.6 us

profile of v6, /device:TPU:0, one launch (start us, length us, event | category | flops | bytes accessed | tf_op | source)
XLA Modules:
  0.0 68.9 jit_solution(4655199438689010100)
XLA Ops:
  0.0 67.6 %em_step.1 = f32[64,128]{1,0:T(8,128)} custom-call(bf16[32768,128]{1,0:T(8,128)(2,1)} %bitcast.18, bf16[192,4096]{1,0:T(8,128)(2,1)} %constant.2.clone.tab, bf16[64,128]{1,0:T(8,128)(2,1)} %bitcast.20, f32[1,512]{1,0:T(1,128)} %bitcast.22, s32[1,128]{1,0:T(1,128)} %bitcast.23, s32[8,128]{1,0:T(8,128)} %bitcast.21), custom_call_target="tpu_custom_call" | custom-call | tf_op jit(solution)/shard_map/em_step/pallas_call | solution.py:380
  67.6 1.4 %copy.11 = f32[1,2,4096]{2,1,0:T(2,128)} copy(f32[1,2,4096]{2,1,0:T(2,128)} %bitcast.19) | data formatting | bytes 65536
